TPU v7x, 32 devices: a whole 2x2x4 slice. The times are simulated.
32 devices in a mesh: orb: 8 (over z, core), bas: 4 (over y, x).
Axes of the slice: x: 2, y: 2, z: 4, core: 2. Of those that a mesh axis runs over, the one named last changes fastest.
Arguments:
- coeffs: bfloat16 [131072, 1024], P('bas', 'orb'), may hold values from -6 to 6
- dipole: bfloat16 [3, 4, 32768, 384], P(None, 'bas', 'orb'), may hold values from -0.0008544922 to 0.0008544922
- tile_cols: int32 [4, 256, 3], P('bas', 'orb'), may hold values from -1 to 31, as said below
- matching: int32 [1, 8], replicated, may hold values from 0 to 7, as said below
Outputs:
- localized: bfloat16 [131072, 1024], P('bas', 'orb')
Inputs may be any that keep to these rules, and one draw needn't show every extreme that they name: `tile_cols`: entry [b, r, s] is the column tile of slot s of row tile r of basis block b, counted within the row tile's group of 32 tiles, or -1 for a padded slot; slot 0 is the row tile itself, and the live slots of a row name distinct tiles. `matching`: each row pairs every block with another block and is its own inverse; the rows are distinct rounds of one round-robin tournament.
All inputs are finite; a program needn't handle non-finite values.
Results may differ from a plain program's by a relative error of at most 0.0047.
Values may be sent and summed in bfloat16 or wider, within the bound.
A program may use at most 192 MiB of HBM per device.

v0:
```python
import jax
import jax.numpy as jnp
from jax import lax
from jax.sharding import PartitionSpec as P

BLK = 128
TILE = 128
SLOTS = 3
SWEEPS = 4


def jacobi_pair(gram):
    highest = lax.Precision.HIGHEST
    half = gram.shape[1] // 2
    positions = jnp.arange(half, dtype=jnp.int32)
    accum = jnp.eye(2 * half, dtype=jnp.float32)
    for sweep_index in range(SWEEPS):
        permute = jnp.equal(positions[None, :], (positions[:, None] + sweep_index) % half).astype(
            jnp.float32
        )
        diag_vals = jnp.diagonal(gram, axis1=1, axis2=2)
        head_vals = diag_vals[:, :half]
        tail_vals = jnp.roll(diag_vals[:, half:], -sweep_index, axis=1)
        off_vals = jnp.diagonal(
            jnp.roll(gram[:, :half, half:], -sweep_index, axis=2), axis1=1, axis2=2
        )
        spread = head_vals - tail_vals
        quad_term = jnp.sum(off_vals * off_vals - 0.25 * spread * spread, axis=0)
        lin_term = jnp.sum(off_vals * spread, axis=0)
        angles = 0.25 * jnp.arctan(lin_term / (jnp.abs(quad_term) + 1.0))
        cosine = jnp.cos(angles)
        sine_part = jnp.sin(angles)
        upper_half = jnp.concatenate([jnp.diag(cosine), -(sine_part[:, None] * permute)], axis=1)
        bottom = jnp.concatenate(
            [permute.T * sine_part[None, :], jnp.diag(jnp.roll(cosine, sweep_index))], axis=1
        )
        rotation = jnp.concatenate([upper_half, bottom], axis=0)
        gram = jnp.einsum(
            "ji,kjl->kil",
            rotation,
            jnp.einsum("kij,jl->kil", gram, rotation, precision=highest),
            precision=highest,
        )
        accum = jnp.dot(accum, rotation, precision=highest)
    return accum


def project_rows(dipole_rows, tile_index, local_rows, blocks):
    group_tiles = tile_index.shape[0]
    tile_rows = local_rows.reshape(group_tiles, TILE, blocks * BLK)
    picked = tile_rows[jnp.maximum(tile_index, 0)]
    picked = jnp.where((tile_index >= 0)[:, :, None, None], picked, jnp.zeros_like(picked))
    picked = picked.reshape(group_tiles, SLOTS * TILE, blocks * BLK)
    moments = jnp.einsum(
        "kraj,rjn->kran", dipole_rows, picked, preferred_element_type=jnp.float32
    ).astype(jnp.bfloat16)
    return moments.reshape(3, group_tiles * TILE, blocks, BLK)


def gram_terms(coef_blocks, moment_blocks, partner, leader, follower):
    raw_gram = jnp.einsum(
        "rbi,krbj->bkij", coef_blocks, moment_blocks, preferred_element_type=jnp.float32
    )
    self_gram = 0.5 * (raw_gram + jnp.swapaxes(raw_gram, 2, 3))
    toward = jnp.einsum(
        "rbi,krbj->bkij",
        coef_blocks,
        moment_blocks[:, :, partner],
        preferred_element_type=jnp.float32,
    )
    cross_gram = 0.5 * (toward[leader] + jnp.swapaxes(toward[follower], 2, 3))
    return (self_gram, cross_gram)


def body(coeffs, dipole, tile_cols, matching):
    local_rows = lax.all_to_all(coeffs, "orb", split_axis=0, concat_axis=1, tiled=True)
    blocks = lax.axis_size("orb")
    my_block = lax.axis_index("orb")
    row_count = local_rows.shape[0]
    dipole_rows = dipole[:, 0].reshape(3, tile_cols.shape[1], TILE, SLOTS * TILE)
    tile_index = tile_cols[0]
    block_ids = jnp.arange(blocks, dtype=jnp.int32)
    partner = matching[0]
    leader = jnp.minimum(block_ids, partner)
    follower = jnp.maximum(block_ids, partner)
    moments = project_rows(dipole_rows, tile_index, local_rows, blocks)
    coef_blocks = local_rows.reshape(row_count, blocks, BLK)
    self_gram, cross_gram = gram_terms(coef_blocks, moments, partner, leader, follower)
    my_leader = leader[my_block]
    entries = jnp.stack([self_gram[leader], self_gram[follower], cross_gram], axis=1)
    summed = lax.psum_scatter(entries, "orb", scatter_dimension=0, tiled=True)[0]
    summed = lax.psum(summed, "bas")
    lead_gram = summed[0]
    follow_gram = summed[1]
    cross_mine = summed[2]
    upper_half = jnp.concatenate([lead_gram, cross_mine], axis=2)
    lower_half = jnp.concatenate([jnp.swapaxes(cross_mine, 1, 2), follow_gram], axis=2)
    rotor = jacobi_pair(jnp.concatenate([upper_half, lower_half], axis=1))
    weight = jnp.where(my_leader == my_block, rotor[:, :BLK], rotor[:, BLK:]).astype(jnp.bfloat16)
    weights = lax.all_gather(weight[None], "orb", axis=0, tiled=True)
    is_lead = (leader == block_ids)[:, None, None]
    self_weight = jnp.where(is_lead, weights[:, :BLK], weights[:, BLK:])
    other_weight = jnp.where(is_lead, weights[:, BLK:], weights[:, :BLK])
    rotated = jnp.einsum(
        "rbj,bjn->rbn", coef_blocks, self_weight, preferred_element_type=jnp.float32
    )
    rotated = rotated + jnp.einsum(
        "rbj,bjn->rbn", coef_blocks[:, partner], other_weight, preferred_element_type=jnp.float32
    )
    local_rows = rotated.astype(jnp.bfloat16).reshape(row_count, blocks * BLK)
    return lax.all_to_all(local_rows, "orb", split_axis=1, concat_axis=0, tiled=True)


def solution(mesh):
    in_specs = (P("bas", "orb"), P(None, "bas", "orb", None), P("bas", "orb", None), P())
    out_specs = P("bas", "orb")
    return jax.shard_map(body, mesh=mesh, in_specs=in_specs, out_specs=out_specs, check_vma=False)
```

profile of v0, /device:TPU:0, one launch (start us, length us, event | category | flops | bytes accessed | tf_op | source)
XLA Modules:
  0.0 981.7 jit_solution(16487530379932482928)
XLA Ops:
  6.5 6.5 all-to-all-start
  14.1 182.9 %all-to-all-done = bf16[8,4096,128]{2,1,0:T(8,128)(2,1)} async-done(((bf16[8,4096,128]{2,1,0:T(8,128)(2,1)}), bf16[8,4096,128]{2,1,0:T(8,128)(2,1)}, u32[]{:S(2)}, u32[]{:S(2)}) %all-to-all-start) | async-done | bytes 8388640 | tf_op jit(solution)/shard_map/all_to_all | solution.py:76
  197.0 10.3 %copy.135 = bf16[4096,8,128]{2,1,0:T(8,128)(2,1)} copy(bf16[4096,8,128]{2,0,1:T(8,128)(2,1)} %bitcast.4) | data formatting | bytes 16777216 | tf_op jit(solution)/shard_map/all_to_all | solution.py:76
  207.3 13.3 %reshape.298 = bf16[32,128,1024]{2,1,0:T(8,128)(2,1)} reshape(bf16[4096,8,128]{2,1,0:T(8,128)(2,1)} %copy.135) | data formatting | bytes 16777216 | tf_op jit(solution)/shard_map/reshape | solution.py:50
  220.6 13.6 %gather_fusion = bf16[96,128,1024]{2,1,0:T(8,128)(2,1)} fusion(bf16[32,128,1024]{2,1,0:T(8,128)(2,1)} %reshape.298, s32[1024]{0:T(1024)S(1)} %pad_clamp_fusion.3), kind=kCustom, calls=%fused_computation | custom fusion | bytes 50332032 | tf_op jit(solution)/shard_map/gather | solution.py:51
  234.2 20.9 %bitcast_select_fusion = bf16[32,384,1024]{2,1,0:T(8,128)(2,1)} fusion(pred[32,384]{1,0:T(8,128)(4,1)S(1)} %bitcast.185, bf16[32,384,1024]{2,1,0:T(8,128)(2,1)} %bitcast.176), kind=kLoop, calls=%fused_computation.22 | loop fusion | flops 12582912 | bytes 50343936 | tf_op jit(solution)/shard_map/jit(_where)/select_n | solution.py:52
  255.1 25.8 %convert_bitcast_fusion = bf16[3,32,128,1024]{2,3,0,1:T(8,128)(2,1)} fusion(bf16[32,384,1024]{2,1,0:T(8,128)(2,1)} %bitcast_select_fusion, bf16[3,32,128,384]{3,2,1,0:T(8,128)(2,1)} %bitcast.200), kind=kOutput, calls=%fused_computation.23 | convolution fusion | flops 9676259328 | bytes 59768832 | tf_op jit(solution)/shard_map/kraj,rjn->kran/dot_general | solution.py:54
  280.9 32.6 %copy.139 = bf16[3,32,128,1024]{3,2,1,0:T(8,128)(2,1)} copy(bf16[3,32,128,1024]{2,3,0,1:T(8,128)(2,1)} %convert_bitcast_fusion) | data formatting | bytes 50331648 | tf_op jit(solution)/shard_map/convert_element_type | solution.py:56
  313.5 23.2 %copy.185 = bf16[1536,8,8,128]{3,2,1,0:T(8,128)(2,1)} copy(bf16[1536,8,8,128]{3,1,2,0:T(8,128)(2,1)} %bitcast.174) | data formatting | bytes 50331648
  336.7 31.7 %copy.140 = bf16[3,4096,8,128]{1,3,0,2:T(8,128)(2,1)} copy(bf16[3,4096,8,128]{3,2,1,0:T(8,128)(2,1)} %bitcast.175) | data formatting | bytes 50331648 | tf_op jit(solution)/shard_map/reshape | solution.py:57
  368.3 17.8 %fusion.95 = (bf16[3,2048,8,128]{1,3,0,2:T(8,128)(2,1)}, bf16[3,2048,8,128]{1,3,0,2:T(8,128)(2,1)}) fusion(bf16[3,4096,8,128]{1,3,0,2:T(8,128)(2,1)} %copy.140), kind=kLoop, calls=%fused_computation.191 | loop fusion | bytes 50331648 | tf_op jit(solution)/shard_map/gather | solution.py:68
  386.1 10.9 %gather_fusion.14 = bf16[8,3,2048,128]{2,3,1,0:T(8,128)(2,1)} fusion(bf16[3,2048,8,128]{1,3,0,2:T(8,128)(2,1)} %get-tuple-element.21, s32[1024]{0:T(1024)S(1)} %get-tuple-element.40), kind=kCustom, calls=%fused_computation.14 | custom fusion | bytes 25165856 | tf_op jit(solution)/shard_map/gather | solution.py:68
  397.0 10.9 %gather_fusion.15 = bf16[8,3,2048,128]{2,3,1,0:T(8,128)(2,1)} fusion(bf16[3,2048,8,128]{1,3,0,2:T(8,128)(2,1)} %get-tuple-element.22, s32[1024]{0:T(1024)S(1)} %get-tuple-element.40), kind=kCustom, calls=%fused_computation.15 | custom fusion | bytes 25165856 | tf_op jit(solution)/shard_map/gather | solution.py:68
  408.0 14.2 %fusion.19 = f32[8,3,128,128]{2,3,1,0:T(8,128)S(1)} fusion(bf16[8,4096,128]{2,1,0:T(8,128)(2,1)} %all-to-all-done, bf16[3,2048,8,128]{1,3,0,2:T(8,128)(2,1)} %bitcast.179, bf16[3,2048,8,128]{1,3,0,2:T(8,128)(2,1)} %bitcast.178), kind=kOutput, calls=%fused_computation.37 | convolution fusion | flops 3271557120 | bytes 35127296 | tf_op jit(solution)/shard_map/rbi,krbj->bkij/dot_general | solution.py:65
  425.6 14.0 %fusion.11 = f32[8,3,128,128]{3,2,1,0:T(8,128)S(1)} fusion(bf16[3,4096,8,128]{1,3,0,2:T(8,128)(2,1)} %copy.140, bf16[8,4096,128]{2,1,0:T(8,128)(2,1)} %all-to-all-done), kind=kOutput, calls=%fused_computation.28 | convolution fusion | flops 3221225472 | bytes 35127296 | tf_op jit(solution)/shard_map/rbi,krbj->bkij/dot_general | solution.py:61
  445.4 3.4 gather_fusion.3
  454.4 104.7 %all-reduce.6.cloned.1.call-done = f32[8,3,3,128,128]{4,3,2,0,1:T(8,128)} async-done(((f32[8,3,3,128,128]{4,3,2,0,1:T(8,128)}), f32[8,3,3,128,128]{4,3,2,0,1:T(8,128)}) %all-reduce.6.cloned.1.call-update) | async-done | bytes 4718608
  563.1 8.5 gather_fusion.13
  571.5 36.7 %all-reduce.4.cloned.1.call-done = f32[3,3,128,128]{3,2,1,0:T(8,128)} async-done(((f32[3,3,128,128]{3,2,1,0:T(8,128)}), f32[3,3,128,128]{3,2,1,0:T(8,128)}) %all-reduce.4.cloned.1.call-update) | async-done | bytes 589840 | tf_op jit(solution)/shard_map/psum | solution.py:92
  609.6 4.6 copy.145
  616.2 16.9 %copy.148 = f32[3,256,256]{0,2,1:T(8,128)} copy(f32[3,256,256]{2,1,0:T(8,128)S(1)} %maximum_maximum_fusion) | data formatting | bytes 1572864 | tf_op jit(solution)/shard_map/concatenate | solution.py:98
  637.9 16.7 %copy.153 = f32[3,256,256]{0,2,1:T(8,128)} copy(f32[3,256,256]{1,2,0:T(8,128)S(1)} %convolution_bitcast_fusion.2) | data formatting | bytes 1572864 | tf_op jit(solution)/shard_map/ji,kjl->kil/transpose | solution.py:38
  657.1 7.5 copy.151
  670.1 16.9 %copy.159 = f32[3,256,256]{0,2,1:T(8,128)} copy(f32[3,256,256]{1,2,0:T(8,128)S(1)} %convolution_bitcast_fusion.1) | data formatting | bytes 1572864 | tf_op jit(solution)/shard_map/ji,kjl->kil/transpose | solution.py:38
  689.5 7.5 copy.157
  701.4 16.7 %copy.165 = f32[3,256,256]{0,2,1:T(8,128)} copy(f32[3,256,256]{1,2,0:T(8,128)S(1)} %convolution_bitcast_fusion) | data formatting | bytes 1572864 | tf_op jit(solution)/shard_map/ji,kjl->kil/transpose | solution.py:38
  720.6 7.5 copy.163
  732.0 15.0 %all-gather = bf16[2048,128]{1,0:T(8,128)(2,1)S(1)} all-gather(bf16[256,128]{1,0:T(8,128)(2,1)S(1)} %fusion.47), channel_id=2, replica_groups=mesh['orb'=8,'bas'=4] {'orb'}, dimensions={0}, use_global_device_ids=true | all-gather | bytes 589824 | tf_op jit(solution)/shard_map/all_gather | solution.py:100
  747.3 11.5 %fusion.42 = f32[8,128,4096]{2,1,0:T(8,128)} fusion(bf16[8,128,128]{1,2,0:T(8,128)(2,1)S(1)} %copy.182, bf16[8,128,128]{1,2,0:T(8,128)(2,1)S(1)} %copy.183, pred[8]{0:T(512)(128)(4,1)S(1)} %iota_compare_fusion.11, bf16[8,4096,128]{2,1,0:T(8,128)(2,1)} %all-to-all-done), kind=kOutput, calls=%fused_computation.64 | convolution fusion | flops 1073872896 | bytes 25690120 | tf_op jit(solution)/shard_map/rbj,bjn->rbn/dot_general | solution.py:104
  758.8 14.0 %fusion.13 = bf16[4096,8,128]{0,2,1:T(8,128)(2,1)} fusion(f32[8,128,4096]{2,1,0:T(8,128)} %fusion.42, bf16[8,4096,128]{2,1,0:T(8,128)(2,1)} %gather_fusion.13, bf16[8,128,128]{1,2,0:T(8,128)(2,1)S(1)} %copy.183, bf16[8,128,128]{1,2,0:T(8,128)(2,1)S(1)} %copy.182, pred[8]{0:T(512)(128)(4,1)S(1)} %iota_compare_fusion.11), kind=kOutput, calls=%fused_computation.30 | convolution fusion | flops 1082261504 | bytes 34078728 | tf_op jit(solution)/shard_map/rbj,bjn->rbn/dot_general | solution.py:107
  772.9 189.9 %all_to_all.32 = bf16[4096,8,128]{0,2,1:T(8,128)(2,1)} all-to-all(bf16[4096,8,128]{0,2,1:T(8,128)(2,1)} %fusion.13), channel_id=1, replica_groups=mesh['orb'=8,'bas'=4] {'orb'}, dimensions={1} | all-to-all | bytes 16777216 | tf_op jit(solution)/shard_map/all_to_all | solution.py:111
  962.7 11.9 %copy.169 = bf16[8,4096,128]{2,1,0:T(8,128)(2,1)} copy(bf16[8,4096,128]{1,2,0:T(8,128)(2,1)} %bitcast.177) | data formatting | bytes 16777216 | tf_op jit(solution)/shard_map/all_to_all | solution.py:111
  (121 shorter events, 48.4 us)
Async XLA Ops:
  6.5 6.5 copy-start.1
  6.5 7.0 copy-start.2
  6.5 190.5 %all-to-all-start = ((bf16[8,4096,128]{2,1,0:T(8,128)(2,1)}), bf16[8,4096,128]{2,1,0:T(8,128)(2,1)}, u32[]{:S(2)}, u32[]{:S(2)}) async-start(bf16[8,4096,128]{2,1,0:T(8,128)(2,1)} %bitcast.180), calls=%async_computation | async-start | bytes 16777216 | tf_op jit(solution)/shard_map/all_to_all | solution.py:76
  13.0 546.1 %all-reduce.6.cloned.1.call-start = ((), (), s32[]{:S(2)}) async-start(), calls=%async_computation.3 | async-start | bytes 9437184
  445.4 5.6 copy-start
  448.9 4.8 copy-start.4
  448.9 5.5 copy-start.3
  453.7 154.6 %all-reduce.4.cloned.1.call-start = ((), (), s32[]{:S(2)}) async-start(), calls=%async_computation.2 | async-start | bytes 1179648 | tf_op jit(solution)/shard_map/psum | solution.py:92
Sparse Core Ops, SparseCore 0:
  453.8 105.2 all-reduce.5
  562.1 46.1 all-reduce.3
where the time goes:
time: 994 us; the launch traced here: 982 us
  waiting for transfers between devices  324 us (33%)
  local copies, waits for them, and re-layouts  315 us (32%)
  blocking collectives  205 us (21%)
  matrix products  86 us (9%)
  other arithmetic  30.6 us (3%)
  between operations  14.9 us (1%)
    all_to_all x1, blocking collectives, body(): lax.all_to_all(local_rows, 'orb', split_axis=1, concat_axis=0, tiled=True)  190 us
    all_to_all x1, waiting for transfers between devices, body(): lax.all_to_all(coeffs, 'orb', split_axis=0, concat_axis=1, tiled=True)  183 us
    unnamed x3, waiting for transfers between devices  105 us
    transpose x3, local copies, waits for them, and re-layouts, jacobi_pair(): jnp.einsum('ji,kjl->kil', rotation, jnp.einsum('kij,jl->kil', gram, rotat...  50.4 us
    gather x3, local copies, waits for them, and re-layouts, gram_terms(): moment_blocks[:, :, partner]  39.6 us
    psum x1, waiting for transfers between devices, body(): summed = lax.psum(summed, 'bas')  36.7 us
    convert_element_type x1, local copies, waits for them, and re-layouts, project_rows(): moments = jnp.einsum('kraj,rjn->kran', dipole_rows, picked, preferred_ele...  32.6 us
    reshape x1, local copies, waits for them, and re-layouts, project_rows(): return moments.reshape(3, group_tiles * TILE, blocks, BLK)  31.7 us
  transfers between devices with their start and end apart: 3, of which 3 were waited for; matrix products, arithmetic and copies ran while one was open for 1% of the time, Pallas kernels for 0%

commit v1 on v0

v1 whole, which is shorter than its diff:
```python
import functools

import jax
import jax.numpy as jnp
from jax import lax
from jax.experimental import pallas as pl
from jax.experimental.pallas import tpu as pltpu
from jax.sharding import PartitionSpec as P

SWEEPS = 4
VMEM_LIMIT = 56 * 1024 * 1024


def permute_kernel(index_ref, in_ref, out_ref):
    out_ref[...] = in_ref[...]


def permute_blocks(blocks, index):
    count, rows, cols = blocks.shape
    return pl.pallas_call(
        permute_kernel,
        out_shape=jax.ShapeDtypeStruct(blocks.shape, blocks.dtype),
        grid_spec=pltpu.PrefetchScalarGridSpec(
            num_scalar_prefetch=1,
            grid=(count,),
            in_specs=[pl.BlockSpec((1, rows, cols), lambda o, index: (index[o], 0, 0))],
            out_specs=pl.BlockSpec((1, rows, cols), lambda o, index: (o, 0, 0)),
        ),
        cost_estimate=pl.CostEstimate(
            flops=0, bytes_accessed=2 * blocks.size * 2, transcendentals=0
        ),
    )(index, blocks)


def pair_kernel(
    tiles, slots, leads, follows, table, lead_ref, follow_ref, dipole_ref, out_ref, x_ref, xt_ref, m_ref
):
    tile = lead_ref.shape[1] // tiles
    half = lead_ref.shape[2]
    x_ref[:, :half] = lead_ref[0]
    x_ref[:, half:] = follow_ref[0]

    def project(r, carry):
        rows = pl.ds(pl.multiple_of(r * tile, tile), tile)
        picked = []
        for s in range(slots):
            col = table[r * slots + s]
            start = pl.multiple_of(jnp.maximum(col, 0) * tile, tile)
            piece = x_ref[pl.ds(start, tile), :]
            picked.append(jnp.where(col >= 0, piece, jnp.zeros_like(piece)))
        picked = jnp.concatenate(picked, axis=0)
        for k in range(3):
            m_ref[k, rows, :] = jnp.dot(
                dipole_ref[k, rows, :], picked, preferred_element_type=jnp.float32
            ).astype(jnp.bfloat16)
        xt_ref[:, rows] = x_ref[rows, :].T
        return carry

    lax.fori_loop(0, tiles, project, 0)
    for k in range(3):
        out_ref[0, k] = jnp.dot(xt_ref[...], m_ref[k], preferred_element_type=jnp.float32)


def pair_grams(local, dipole, table, leads, follows):
    blocks, rows, half = local.shape
    tiles, slots = table.shape
    pairs = blocks // 2
    flops = pairs * 2 * 3 * rows * 2 * half * (dipole.shape[2] + 2 * half)
    return pl.pallas_call(
        functools.partial(pair_kernel, tiles, slots),
        out_shape=jax.ShapeDtypeStruct((pairs, 3, 2 * half, 2 * half), jnp.float32),
        grid_spec=pltpu.PrefetchScalarGridSpec(
            num_scalar_prefetch=3,
            grid=(pairs,),
            in_specs=[
                pl.BlockSpec((1, rows, half), lambda q, lead, follow, t: (lead[q], 0, 0)),
                pl.BlockSpec((1, rows, half), lambda q, lead, follow, t: (follow[q], 0, 0)),
                pl.BlockSpec(dipole.shape, lambda q, lead, follow, t: (0, 0, 0)),
            ],
            out_specs=pl.BlockSpec(
                (1, 3, 2 * half, 2 * half), lambda q, lead, follow, t: (q, 0, 0, 0)
            ),
            scratch_shapes=[
                pltpu.VMEM((rows, 2 * half), jnp.bfloat16),
                pltpu.VMEM((2 * half, rows), jnp.bfloat16),
                pltpu.VMEM((3, rows, 2 * half), jnp.bfloat16),
            ],
        ),
        compiler_params=pltpu.CompilerParams(vmem_limit_bytes=VMEM_LIMIT),
        cost_estimate=pl.CostEstimate(
            flops=flops, bytes_accessed=2 * (local.size + dipole.size), transcendentals=0
        ),
    )(leads, follows, table.reshape(-1), local, local, dipole)


def arctan(x):
    mag = jnp.abs(x)
    big = mag > 2.414213562373095
    mid = mag > 0.4142135623730950
    num = jnp.where(big, -1.0, jnp.where(mid, mag - 1.0, mag))
    den = jnp.where(big, mag, jnp.where(mid, mag + 1.0, 1.0))
    base = jnp.where(big, 1.5707963267948966, jnp.where(mid, 0.7853981633974483, 0.0))
    t = num / den
    w = t * t
    poly = ((8.05374449538e-2 * w - 1.38776856032e-1) * w + 1.99777106478e-1) * w
    poly = (poly - 3.33329491539e-1) * w * t + t
    out = base + poly
    return jnp.where(x < 0, -out, out)


def jacobi_kernel(in_ref, out_ref):
    half = in_ref.shape[2] // 2
    rows = lax.broadcasted_iota(jnp.int32, (half, half), 0)
    cols = lax.broadcasted_iota(jnp.int32, (half, half), 1)
    eye = rows == cols
    quads = []
    for k in range(3):
        full = in_ref[0, k]
        full = 0.5 * (full + full.T)
        quads.append(
            [full[:half, :half], full[:half, half:], full[half:, :half], full[half:, half:]]
        )
    one = jnp.where(eye, 1.0, 0.0).astype(jnp.float32)
    zero = jnp.zeros((half, half), jnp.float32)
    rotor = [one, zero, zero, one]

    def angles(axis):
        quad_term = lin_term = 0.0
        for ll, lf, _, ff in quads:
            head, off, tail = (
                jnp.sum(jnp.where(eye, v, 0.0), axis=axis, keepdims=True) for v in (ll, lf, ff)
            )
            spread = head - tail
            quad_term = quad_term + (off * off - 0.25 * spread * spread)
            lin_term = lin_term + off * spread
        theta = 0.25 * arctan(lin_term / (jnp.abs(quad_term) + 1.0))
        return jnp.cos(theta), jnp.sin(theta)

    for sweep in range(SWEEPS):
        if sweep:
            back = half - 1
            for q in quads:
                q[1] = pltpu.roll(q[1], back, 1)
                q[2] = pltpu.roll(q[2], back, 0)
                q[3] = pltpu.roll(pltpu.roll(q[3], back, 1), back, 0)
            rotor[1] = pltpu.roll(rotor[1], back, 1)
            rotor[3] = pltpu.roll(rotor[3], back, 1)
        row_cos, row_sin = angles(0)
        col_cos, col_sin = angles(1)
        for i, (ll, lf, fl, ff) in enumerate(quads):
            ll, lf = ll * row_cos + lf * row_sin, lf * row_cos - ll * row_sin
            fl, ff = fl * row_cos + ff * row_sin, ff * row_cos - fl * row_sin
            ll, fl = ll * col_cos + fl * col_sin, fl * col_cos - ll * col_sin
            lf, ff = lf * col_cos + ff * col_sin, ff * col_cos - lf * col_sin
            quads[i] = [ll, lf, fl, ff]
        ll, lf, fl, ff = rotor
        rotor = [
            ll * row_cos + lf * row_sin,
            lf * row_cos - ll * row_sin,
            fl * row_cos + ff * row_sin,
            ff * row_cos - fl * row_sin,
        ]
    lf, ff = (pltpu.roll(v, SWEEPS - 1, 1) for v in (rotor[1], rotor[3]))
    out_ref[0, :half, :half] = rotor[0].astype(jnp.bfloat16)
    out_ref[0, half:, :half] = rotor[2].astype(jnp.bfloat16)
    out_ref[0, :half, half:] = lf.astype(jnp.bfloat16)
    out_ref[0, half:, half:] = ff.astype(jnp.bfloat16)


def jacobi(grams):
    pairs, _, size, _ = grams.shape
    return pl.pallas_call(
        jacobi_kernel,
        out_shape=jax.ShapeDtypeStruct((pairs, size, size), jnp.bfloat16),
        grid=(pairs,),
        in_specs=[pl.BlockSpec((1, 3, size, size), lambda q: (q, 0, 0, 0))],
        out_specs=pl.BlockSpec((1, size, size), lambda q: (q, 0, 0)),
        compiler_params=pltpu.CompilerParams(vmem_limit_bytes=32 * 1024 * 1024),
        cost_estimate=pl.CostEstimate(
            flops=pairs * SWEEPS * 3 * 12 * size * size,
            bytes_accessed=grams.size * 4,
            transcendentals=pairs * SWEEPS * 4 * size,
        ),
    )(grams)


def rotate_kernel(own_ref, other_ref, weight_ref, out_ref):
    both = jnp.concatenate([own_ref[...], other_ref[...]], axis=1)
    out_ref[...] = jnp.dot(both, weight_ref[...], preferred_element_type=jnp.float32).astype(
        jnp.bfloat16
    )


def rotate(own, other, weight):
    rows, half = own.shape
    step = min(rows, 4096)
    return pl.pallas_call(
        rotate_kernel,
        out_shape=jax.ShapeDtypeStruct(own.shape, own.dtype),
        grid=(rows // step,),
        in_specs=[
            pl.BlockSpec((step, half), lambda i: (i, 0)),
            pl.BlockSpec((step, half), lambda i: (i, 0)),
            pl.BlockSpec((2 * half, half), lambda i: (0, 0)),
        ],
        out_specs=pl.BlockSpec((step, half), lambda i: (i, 0)),
        compiler_params=pltpu.CompilerParams(vmem_limit_bytes=32 * 1024 * 1024),
        cost_estimate=pl.CostEstimate(
            flops=4 * rows * half * half, bytes_accessed=6 * own.size, transcendentals=0
        ),
    )(own, other, weight)


def body(coeffs, dipole, tile_cols, matching):
    blocks = lax.axis_size("orb")
    me = lax.axis_index("orb")
    rows, half = coeffs.shape
    pairs = blocks // 2
    block_ids = jnp.arange(blocks, dtype=jnp.int32)
    partner = matching[0]
    is_lead = block_ids < partner
    before = is_lead[None, :] & (block_ids[None, :] < block_ids[:, None])
    rank = jnp.sum(before.astype(jnp.int32), axis=1)
    chosen = is_lead[None, :] & (rank[None, :] == jnp.arange(pairs, dtype=jnp.int32)[:, None])
    leads = jnp.sum(jnp.where(chosen, block_ids[None, :], 0), axis=1)
    follows = jnp.sum(jnp.where(chosen, partner[None, :], 0), axis=1)

    local = lax.all_to_all(
        coeffs.reshape(blocks, rows // blocks, half), "orb", split_axis=0, concat_axis=0
    )
    swapped = permute_blocks(local, partner)
    other = lax.all_to_all(swapped, "orb", split_axis=0, concat_axis=0).reshape(rows, half)

    grams = pair_grams(local, dipole[:, 0], tile_cols[0], leads, follows)
    grams = lax.psum_scatter(grams, "bas", scatter_dimension=0, tiled=True)
    grams = lax.psum(grams, "orb")
    rotors = lax.all_gather(jacobi(grams), "bas", axis=0, tiled=True)
    mine = (leads == me) | (follows == me)
    rotor = jnp.sum(jnp.where(mine[:, None, None], rotors, jnp.zeros_like(rotors)), axis=0)
    leading = jnp.any(leads == me)
    weight = jnp.where(
        leading,
        rotor[:, :half],
        jnp.concatenate([rotor[half:, half:], rotor[:half, half:]], axis=0),
    )
    return rotate(coeffs, other, weight)


def solution(mesh):
    in_specs = (P("bas", "orb"), P(None, "bas", "orb", None), P("bas", "orb", None), P())
    out_specs = P("bas", "orb")
    return jax.shard_map(body, mesh=mesh, in_specs=in_specs, out_specs=out_specs, check_vma=False)
```

time: 994 us -> 448 us (0.45); the launches traced: 982 us -> 448 us
  local copies, waits for them, and re-layouts: 315 us -> 5.24 us
  waiting for transfers between devices: 324 us -> 146 us
  matrix products: 86 us -> 0 us
  Pallas kernels: 0 us -> 74.2 us
  other arithmetic: 30.6 us -> 2.06 us
    all_to_all x1, waiting for transfers between devices: 183 us -> 0.01 us  [body(): lax.all_to_all(swapped, 'orb', split_axis=0, concat_axis=0)]
    gather x25 -> x0, local copies, waits for them, and re-layouts: 86.9 us -> none  [the longest x3 39.6 us: gram_terms(): moment_blocks[:, :, partner]]
    dot_general x15 -> x0, matrix products: 86 us -> none  [the longest x1 25.8 us: project_rows(): jnp.einsum('kraj,rjn->kran', dipole_rows, picked, preferred_element_type=...]
    pallas_call x0 -> x4, Pallas kernels: none -> 74.2 us  [the longest x1 50.9 us: pair_grams(): pl.pallas_call(functools.partial(pair_kernel, tiles, slots), out_shape=ja...]
    psum x1, waiting for transfers between devices: 36.7 us -> 99.7 us  [body(): grams = lax.psum(grams, 'orb')]
    unnamed x3, waiting for transfers between devices: 105 us -> 46.3 us
    transpose x5 -> x0, local copies, waits for them, and re-layouts: 52.1 us -> none  [the longest x3 50.4 us: jacobi_pair(): jnp.einsum('ji,kjl->kil', rotation, jnp.einsum('kij,jl->kil', gram, rotat...]
    reshape x2 -> x0, local copies, waits for them, and re-layouts: 45 us -> none  [the longest x1 31.7 us: project_rows(): return moments.reshape(3, group_tiles * TILE, blocks, BLK)]
  transfers between devices with their start and end apart: 3 -> 3, of which waited for: 3 -> 2; matrix products, arithmetic and copies ran while one was open for 1% -> 1% of each run, Pallas kernels for 0% -> 12%
where the time goes in v1:
time: 448 us
  blocking collectives  201 us (45%)
  waiting for transfers between devices  146 us (33%)
  Pallas kernels  74.2 us (17%)
  between operations  13.5 us (3%)
  local copies, waits for them, and re-layouts  5.24 us (1%)
  starting transfers between devices  5.18 us (1%)
    all_to_all x1, blocking collectives, body(): lax.all_to_all(coeffs.reshape(blocks, rows // blocks, half), 'orb', split...  190 us
    psum x1, waiting for transfers between devices, body(): grams = lax.psum(grams, 'orb')  99.7 us
    pallas_call x1, Pallas kernels, pair_grams(): pl.pallas_call(functools.partial(pair_kernel, tiles, slots), out_shape=ja...  50.9 us
    unnamed x3, waiting for transfers between devices  46.3 us
    all_gather x1, blocking collectives, body(): rotors = lax.all_gather(jacobi(grams), 'bas', axis=0, tiled=True)  11 us
    pallas_call x1, Pallas kernels, rotate(): pl.pallas_call(rotate_kernel, out_shape=jax.ShapeDtypeStruct(own.shape, o...  10.8 us
    pallas_call x1, Pallas kernels, permute_blocks(): pl.pallas_call(permute_kernel, out_shape=jax.ShapeDtypeStruct(blocks.shap...  9.65 us
  transfers between devices with their start and end apart: 3, of which 2 were waited for; matrix products, arithmetic and copies ran while one was open for 1% of the time, Pallas kernels for 12%

profile of v1, /device:TPU:0, one launch (start us, length us, event | category | flops | bytes accessed | tf_op | source)
XLA Modules:
  0.0 447.6 jit_solution(17846234946865381126)
XLA Ops:
  6.5 190.4 %all_to_all.10.in_ref.lead_ref.follow_ref = bf16[8,4096,128]{2,1,0:T(8,128)(2,1)} all-to-all(bf16[8,4096,128]{2,1,0:T(8,128)(2,1)} %bitcast.7), channel_id=1, replica_groups=mesh['orb'=8,'bas'=4] {'orb'}, dimensions={0} | all-to-all | bytes 16777216 | tf_op jit(solution)/shard_map/all_to_all | solution.py:228
  196.9 9.6 %shard_map.46 = bf16[8,4096,128]{2,1,0:T(8,128)(2,1)} custom-call(s32[8]{0:T(128)} %bitcast.8, bf16[8,4096,128]{2,1,0:T(8,128)(2,1)} %all_to_all.10.in_ref.lead_ref.follow_ref), custom_call_target="tpu_custom_call" | custom-call | bytes 16777216 | tf_op jit(solution)/shard_map/pallas_call | solution.py:20
  206.6 0.0 copy-start.5
  206.6 0.0 copy-start.2
  206.6 5.1 %all-to-all-start.1 = ((bf16[8,4096,128]{2,1,0:T(8,128)(2,1)}), bf16[8,4096,128]{2,1,0:T(8,128)(2,1)}, u32[]{:S(2)}, u32[]{:S(2)}) async-start(bf16[8,4096,128]{2,1,0:T(8,128)(2,1)} %shard_map.46), calls=%async_computation.1 | async-start | bytes 16777216 | tf_op jit(solution)/shard_map/all_to_all | solution.py:232
  211.7 0.0 reduce-scatter.4.cloned.1.call-start
  211.7 0.0 copy-done.5
  211.8 0.1 copy.8
  211.8 0.6 reshape_squeeze.3.table
  212.5 0.0 copy-done.2
  212.5 0.1 convert_reduce_fusion
  212.6 0.6 select_reduce_fusion.1
  213.2 0.0 copy-start.3
  213.2 0.0 copy-start.4
  213.2 50.9 %shard_map.47 = f32[4,3,256,256]{3,2,1,0:T(8,128)} custom-call(s32[4]{0:T(128)} %get-tuple-element.6.leads, s32[4]{0:T(128)} %get-tuple-element.5.follows, s32[96]{0:T(128)} %reshape_squeeze.3.table, bf16[8,4096,128]{2,1,0:T(8,128)(2,1)} %all_to_all.10.in_ref.lead_ref.follow_ref, bf16[8,4096,128]{2,1,0:T(8,128)(2,1)} %all_to_all.10.in_ref.lead_ref.follow_ref, ...), custom_call_target="tpu_custom_call" | custom-call | flops 16106127360 | bytes 17825792 | tf_op jit(solution)/shard_map/pallas_call | solution.py:69
  264.1 0.0 reduce-scatter.4.cloned.1.call-update
  264.1 0.0 all-reduce.3.cloned.1.call-start
  264.2 46.3 %reduce-scatter.4.cloned.1.call-done = f32[1,3,256,256]{3,2,1,0:T(8,128)} async-done(((f32[4,3,256,256]{3,2,1,0:T(8,128)}), f32[1,3,256,256]{3,2,1,0:T(8,128)}) %reduce-scatter.4.cloned.1.call-update) | async-done | bytes 786448
  310.5 0.0 all-reduce.3.cloned.1.call-update
  310.5 0.0 copy-done.3
  310.5 0.0 copy-done.4
  310.6 0.6 compare_reduce_fusion
  311.2 99.7 %all-reduce.3.cloned.1.call-done.in_ref = f32[1,3,256,256]{3,2,1,0:T(8,128)} async-done(((f32[1,3,256,256]{3,2,1,0:T(8,128)}), f32[1,3,256,256]{3,2,1,0:T(8,128)}) %all-reduce.3.cloned.1.call-update) | async-done | bytes 786448 | tf_op jit(solution)/shard_map/psum | solution.py:236
  410.9 1.1 copy-done.1
  412.0 2.9 shard_map.48
  414.9 11.0 %all_gather.3 = bf16[4,256,256]{2,1,0:T(8,128)(2,1)S(1)} all-gather(bf16[1,256,256]{2,1,0:T(8,128)(2,1)S(1)} %shard_map.48), channel_id=1, replica_groups=mesh['orb'=8,'bas'=4] {'bas'}, dimensions={0}, use_global_device_ids=true | all-gather | bytes 655360 | tf_op jit(solution)/shard_map/all_gather | solution.py:237
  425.9 0.1 select_reduce_fusion
  426.0 0.6 slice_select_fusion.weight_ref
  426.6 0.0 all-to-all-done.1
  426.6 0.0 copy-start
  426.6 3.4 copy-done
  430.0 10.8 %shard_map.49 = bf16[32768,128]{1,0:T(8,128)(2,1)} custom-call(bf16[32768,128]{1,0:T(8,128)(2,1)S(1)} %copy-done, bf16[32768,128]{1,0:T(8,128)(2,1)} %bitcast.2.other_ref, bf16[256,128]{1,0:T(8,128)(2,1)S(1)} %slice_select_fusion.weight_ref), custom_call_target="tpu_custom_call" | custom-call | flops 2147483648 | bytes 25165824 | tf_op jit(solution)/shard_map/pallas_call | solution.py:197
  (3 shorter events, 0.0 us)
Async XLA Ops:
  206.6 5.2 %copy-start.5 = (s32[1,32,3]{1,0,2:T(1,128)S(1)}, s32[1,32,3]{1,0,2:T(1,128)}, u32[]{:S(2)}) copy-start(s32[1,32,3]{1,0,2:T(1,128)} %param.6) | copy-start | bytes 1156
  206.6 5.9 %copy-start.2 = (s32[1,8]{1,0:T(1,128)S(1)}, s32[1,8]{1,0:T(1,128)}, u32[]{:S(2)}) copy-start(s32[1,8]{1,0:T(1,128)} %param.7) | copy-start | bytes 100
  206.6 220.0 %all-to-all-start.1 = ((bf16[8,4096,128]{2,1,0:T(8,128)(2,1)}), bf16[8,4096,128]{2,1,0:T(8,128)(2,1)}, u32[]{:S(2)}, u32[]{:S(2)}) async-start(bf16[8,4096,128]{2,1,0:T(8,128)(2,1)} %shard_map.46), calls=%async_computation.1 | async-start | bytes 16777216 | tf_op jit(solution)/shard_map/all_to_all | solution.py:232
  211.7 98.8 %reduce-scatter.4.cloned.1.call-start = ((), (), s32[]{:S(2)}) async-start(), calls=%async_computation.4 | async-start | bytes 3932160
  213.2 97.3 %copy-start.3 = (s32[4]{0:T(128)S(1)}, s32[4]{0:T(128)}, u32[]{:S(2)}) copy-start(s32[4]{0:T(128)} %get-tuple-element.5.follows) | copy-start | bytes 52
  213.2 97.3 %copy-start.4 = (s32[4]{0:T(128)S(1)}, s32[4]{0:T(128)}, u32[]{:S(2)}) copy-start(s32[4]{0:T(128)} %get-tuple-element.6.leads) | copy-start | bytes 52
  264.1 146.7 %all-reduce.3.cloned.1.call-start = ((), (), s32[]{:S(2)}) async-start(), calls=%async_computation.3 | async-start | bytes 1572864 | tf_op jit(solution)/shard_map/psum | solution.py:236
  410.9 1.1 copy-start.1
  426.6 3.4 copy-start
Sparse Core Ops, SparseCore 0:
  264.3 46.1 reduce-scatter.3
  312.9 97.9 all-reduce.2

commit v2 on v1

--- a/solution.py
+++ b/solution.py
@@ -22,10 +22,11 @@
         out_shape=jax.ShapeDtypeStruct(blocks.shape, blocks.dtype),
         grid_spec=pltpu.PrefetchScalarGridSpec(
             num_scalar_prefetch=1,
-            grid=(count,),
-            in_specs=[pl.BlockSpec((1, rows, cols), lambda o, index: (index[o], 0, 0))],
-            out_specs=pl.BlockSpec((1, rows, cols), lambda o, index: (o, 0, 0)),
-        ),
+            grid=(count, 2),
+            in_specs=[pl.BlockSpec((1, rows // 2, cols), lambda o, i, index: (index[o], i, 0))],
+            out_specs=pl.BlockSpec((1, rows // 2, cols), lambda o, i, index: (o, i, 0)),
+        ),
+        compiler_params=pltpu.CompilerParams(vmem_limit_bytes=VMEM_LIMIT),
         cost_estimate=pl.CostEstimate(
             flops=0, bytes_accessed=2 * blocks.size * 2, transcendentals=0
         ),
@@ -49,16 +50,29 @@
             piece = x_ref[pl.ds(start, tile), :]
             picked.append(jnp.where(col >= 0, piece, jnp.zeros_like(piece)))
         picked = jnp.concatenate(picked, axis=0)
+        stacked = jnp.concatenate([dipole_ref[k, rows, :] for k in range(3)], axis=0)
+        moments = jnp.dot(stacked, picked, preferred_element_type=jnp.float32)
+        moments = moments.astype(jnp.bfloat16)
         for k in range(3):
-            m_ref[k, rows, :] = jnp.dot(
-                dipole_ref[k, rows, :], picked, preferred_element_type=jnp.float32
-            ).astype(jnp.bfloat16)
+            m_ref[k, rows, :] = moments[k * tile : (k + 1) * tile]
         xt_ref[:, rows] = x_ref[rows, :].T
         return carry
 
-    lax.fori_loop(0, tiles, project, 0)
+    lax.fori_loop(0, tiles, project, 0, unroll=4)
+    upper = lax.broadcasted_iota(jnp.int32, (half, half), 0) <= lax.broadcasted_iota(
+        jnp.int32, (half, half), 1
+    )
+    eye = lax.broadcasted_iota(jnp.int32, (half, half), 0) == lax.broadcasted_iota(
+        jnp.int32, (half, half), 1
+    )
     for k in range(3):
-        out_ref[0, k] = jnp.dot(xt_ref[...], m_ref[k], preferred_element_type=jnp.float32)
+        gram = jnp.dot(xt_ref[...], m_ref[k], preferred_element_type=jnp.float32)
+        gram = 0.5 * (gram + gram.T)
+        tail = gram[half:, half:]
+        diag = jnp.sum(jnp.where(eye, tail, 0.0), axis=0, keepdims=True)
+        out_ref[0, k, :half] = gram[:half, half:]
+        out_ref[0, k, half : 2 * half] = jnp.where(upper, gram[:half, :half], tail)
+        out_ref[0, k, 2 * half :] = jnp.broadcast_to(diag, (8, half))
 
 
 def pair_grams(local, dipole, table, leads, follows):
@@ -68,7 +82,7 @@
     flops = pairs * 2 * 3 * rows * 2 * half * (dipole.shape[2] + 2 * half)
     return pl.pallas_call(
         functools.partial(pair_kernel, tiles, slots),
-        out_shape=jax.ShapeDtypeStruct((pairs, 3, 2 * half, 2 * half), jnp.float32),
+        out_shape=jax.ShapeDtypeStruct((pairs, 3, 2 * half + 8, half), jnp.float32),
         grid_spec=pltpu.PrefetchScalarGridSpec(
             num_scalar_prefetch=3,
             grid=(pairs,),
@@ -78,7 +92,7 @@
                 pl.BlockSpec(dipole.shape, lambda q, lead, follow, t: (0, 0, 0)),
             ],
             out_specs=pl.BlockSpec(
-                (1, 3, 2 * half, 2 * half), lambda q, lead, follow, t: (q, 0, 0, 0)
+                (1, 3, 2 * half + 8, half), lambda q, lead, follow, t: (q, 0, 0, 0)
             ),
             scratch_shapes=[
                 pltpu.VMEM((rows, 2 * half), jnp.bfloat16),
@@ -109,17 +123,19 @@
 
 
 def jacobi_kernel(in_ref, out_ref):
-    half = in_ref.shape[2] // 2
+    half = in_ref.shape[3]
     rows = lax.broadcasted_iota(jnp.int32, (half, half), 0)
     cols = lax.broadcasted_iota(jnp.int32, (half, half), 1)
     eye = rows == cols
     quads = []
     for k in range(3):
-        full = in_ref[0, k]
-        full = 0.5 * (full + full.T)
-        quads.append(
-            [full[:half, :half], full[:half, half:], full[half:, :half], full[half:, half:]]
-        )
+        cross = in_ref[0, k, :half]
+        mixed = in_ref[0, k, half : 2 * half]
+        flipped = mixed.T
+        head = jnp.where(rows <= cols, mixed, flipped)
+        tail = jnp.where(rows > cols, mixed, flipped)
+        tail = jnp.where(eye, in_ref[0, k, 2 * half : 2 * half + 1], tail)
+        quads.append([head, cross, cross.T, tail])
     one = jnp.where(eye, 1.0, 0.0).astype(jnp.float32)
     zero = jnp.zeros((half, half), jnp.float32)
     rotor = [one, zero, zero, one]
@@ -168,12 +184,13 @@
 
 
 def jacobi(grams):
-    pairs, _, size, _ = grams.shape
+    pairs, _, packed, half = grams.shape
+    size = 2 * half
     return pl.pallas_call(
         jacobi_kernel,
         out_shape=jax.ShapeDtypeStruct((pairs, size, size), jnp.bfloat16),
         grid=(pairs,),
-        in_specs=[pl.BlockSpec((1, 3, size, size), lambda q: (q, 0, 0, 0))],
+        in_specs=[pl.BlockSpec((1, 3, packed, half), lambda q: (q, 0, 0, 0))],
         out_specs=pl.BlockSpec((1, size, size), lambda q: (q, 0, 0)),
         compiler_params=pltpu.CompilerParams(vmem_limit_bytes=32 * 1024 * 1024),
         cost_estimate=pl.CostEstimate(
@@ -193,7 +210,7 @@
 
 def rotate(own, other, weight):
     rows, half = own.shape
-    step = min(rows, 4096)
+    step = min(rows, 2048)
     return pl.pallas_call(
         rotate_kernel,
         out_shape=jax.ShapeDtypeStruct(own.shape, own.dtype),
@@ -204,7 +221,7 @@
             pl.BlockSpec((2 * half, half), lambda i: (0, 0)),
         ],
         out_specs=pl.BlockSpec((step, half), lambda i: (i, 0)),
-        compiler_params=pltpu.CompilerParams(vmem_limit_bytes=32 * 1024 * 1024),
+        compiler_params=pltpu.CompilerParams(vmem_limit_bytes=VMEM_LIMIT),
         cost_estimate=pl.CostEstimate(
             flops=4 * rows * half * half, bytes_accessed=6 * own.size, transcendentals=0
         ),

time: 448 us -> 449 us (level)
  waiting for transfers between devices: 146 us -> 157 us
  Pallas kernels: 74.2 us -> 66 us
    psum x1, waiting for transfers between devices: 99.7 us -> 123 us  [body(): grams = lax.psum(grams, 'orb')]
    pallas_call x1, Pallas kernels: 50.9 us -> 34.3 us  [pair_grams(): pl.pallas_call(functools.partial(pair_kernel, tiles, slots), out_shape=ja...]
    unnamed x3, waiting for transfers between devices: 46.3 us -> 34 us
    pallas_call x1, Pallas kernels: 10.8 us -> 16.4 us  [rotate(): pl.pallas_call(rotate_kernel, out_shape=jax.ShapeDtypeStruct(own.shape, o...]
  transfers between devices with their start and end apart: 3 -> 3, of which waited for: 2 -> 2; matrix products, arithmetic and copies ran while one was open for 1% -> 1% of each run, Pallas kernels for 12% -> 8%
where the time goes in v2:
time: 449 us; the launch traced here: 448 us
  blocking collectives  201 us (45%)
  waiting for transfers between devices  157 us (35%)
  Pallas kernels  66 us (15%)
  between operations  13.5 us (3%)
  starting transfers between devices  5.18 us (1%)
    all_to_all x1, blocking collectives, body(): lax.all_to_all(coeffs.reshape(blocks, rows // blocks, half), 'orb', split...  190 us
    psum x1, waiting for transfers between devices, body(): grams = lax.psum(grams, 'orb')  123 us
    pallas_call x1, Pallas kernels, pair_grams(): pl.pallas_call(functools.partial(pair_kernel, tiles, slots), out_shape=ja...  34.3 us
    unnamed x3, waiting for transfers between devices  34 us
    pallas_call x1, Pallas kernels, rotate(): pl.pallas_call(rotate_kernel, out_shape=jax.ShapeDtypeStruct(own.shape, o...  16.4 us
    pallas_call x1, Pallas kernels, permute_blocks(): pl.pallas_call(permute_kernel, out_shape=jax.ShapeDtypeStruct(blocks.shap...  12.6 us
    all_gather x1, blocking collectives, body(): rotors = lax.all_gather(jacobi(grams), 'bas', axis=0, tiled=True)  11 us
  transfers between devices with their start and end apart: 3, of which 2 were waited for; matrix products, arithmetic and copies ran while one was open for 1% of the time, Pallas kernels for 8%

profile of v2, /device:TPU:0, one launch (start us, length us, event | category | flops | bytes accessed | tf_op | source)
XLA Modules:
  0.0 447.9 jit_solution(11686804292451256531)
XLA Ops:
  6.5 190.4 %all_to_all.10.in_ref.lead_ref.follow_ref = bf16[8,4096,128]{2,1,0:T(8,128)(2,1)} all-to-all(bf16[8,4096,128]{2,1,0:T(8,128)(2,1)} %bitcast.7), channel_id=1, replica_groups=mesh['orb'=8,'bas'=4] {'orb'}, dimensions={0} | all-to-all | bytes 16777216 | tf_op jit(solution)/shard_map/all_to_all | solution.py:245
  196.9 12.6 %shard_map.46 = bf16[8,4096,128]{2,1,0:T(8,128)(2,1)} custom-call(s32[8]{0:T(128)} %bitcast.8, bf16[8,4096,128]{2,1,0:T(8,128)(2,1)} %all_to_all.10.in_ref.lead_ref.follow_ref), custom_call_target="tpu_custom_call" | custom-call | bytes 16777216 | tf_op jit(solution)/shard_map/pallas_call | solution.py:20
  209.5 0.0 copy-start.4
  209.5 0.0 copy-start.1
  209.5 5.1 %all-to-all-start.1 = ((bf16[8,4096,128]{2,1,0:T(8,128)(2,1)}), bf16[8,4096,128]{2,1,0:T(8,128)(2,1)}, u32[]{:S(2)}, u32[]{:S(2)}) async-start(bf16[8,4096,128]{2,1,0:T(8,128)(2,1)} %shard_map.46), calls=%async_computation.1 | async-start | bytes 16777216 | tf_op jit(solution)/shard_map/all_to_all | solution.py:249
  214.6 0.0 reduce-scatter.4.cloned.1.call-start
  214.7 0.0 copy-done.4
  214.7 0.1 copy.8
  214.8 0.6 reshape_squeeze.3.table
  215.4 0.0 copy-done.1
  215.4 0.1 convert_reduce_fusion
  215.5 0.8 select_reduce_fusion.1
  216.2 0.0 copy-start.2
  216.2 0.0 copy-start.3
  216.2 34.3 %shard_map.47 = f32[4,3,264,128]{3,2,1,0:T(8,128)} custom-call(s32[4]{0:T(128)} %get-tuple-element.6.leads, s32[4]{0:T(128)} %get-tuple-element.5.follows, s32[96]{0:T(128)} %reshape_squeeze.3.table, bf16[8,4096,128]{2,1,0:T(8,128)(2,1)} %all_to_all.10.in_ref.lead_ref.follow_ref, bf16[8,4096,128]{2,1,0:T(8,128)(2,1)} %all_to_all.10.in_ref.lead_ref.follow_ref, ...), custom_call_target="tpu_custom_call" | custom-call | flops 16106127360 | bytes 17825792 | tf_op jit(solution)/shard_map/pallas_call | solution.py:83
  250.5 0.0 reduce-scatter.4.cloned.1.call-update
  250.5 0.0 all-reduce.3.cloned.1.call-start
  250.6 33.9 %reduce-scatter.4.cloned.1.call-done = f32[1,3,264,128]{3,2,1,0:T(8,128)} async-done(((f32[4,3,264,128]{3,2,1,0:T(8,128)}), f32[1,3,264,128]{3,2,1,0:T(8,128)}) %reduce-scatter.4.cloned.1.call-update) | async-done | bytes 405520
  284.5 0.0 all-reduce.3.cloned.1.call-update
  284.5 0.0 copy-done.2
  284.6 0.0 copy-done.3
  284.6 0.7 compare_reduce_fusion
  285.3 123.1 %all-reduce.3.cloned.1.call-done.in_ref = f32[1,3,264,128]{3,2,1,0:T(8,128)} async-done(((f32[1,3,264,128]{3,2,1,0:T(8,128)}), f32[1,3,264,128]{3,2,1,0:T(8,128)}) %all-reduce.3.cloned.1.call-update) | async-done | bytes 405520 | tf_op jit(solution)/shard_map/psum | solution.py:253
  408.4 0.0 copy-start
  408.4 1.0 copy-done
  409.4 2.7 shard_map.48
  412.1 11.0 %all_gather.3 = bf16[4,256,256]{2,1,0:T(8,128)(2,1)S(1)} all-gather(bf16[1,256,256]{2,1,0:T(8,128)(2,1)S(1)} %shard_map.48), channel_id=1, replica_groups=mesh['orb'=8,'bas'=4] {'bas'}, dimensions={0}, use_global_device_ids=true | all-gather | bytes 655360 | tf_op jit(solution)/shard_map/all_gather | solution.py:254
  423.1 0.1 select_reduce_fusion
  423.3 1.3 slice_select_fusion.weight_ref
  424.6 0.0 all-to-all-done.1
  424.6 16.4 %shard_map.49 = bf16[32768,128]{1,0:T(8,128)(2,1)} custom-call(bf16[32768,128]{1,0:T(8,128)(2,1)} %own_ref.1, bf16[32768,128]{1,0:T(8,128)(2,1)} %bitcast.2.other_ref, bf16[256,128]{1,0:T(8,128)(2,1)} %slice_select_fusion.weight_ref), custom_call_target="tpu_custom_call" | custom-call | flops 2147483648 | bytes 25165824 | tf_op jit(solution)/shard_map/pallas_call | solution.py:214
  (2 shorter events, 0.0 us)
Async XLA Ops:
  209.5 5.2 %copy-start.4 = (s32[1,32,3]{1,0,2:T(1,128)S(1)}, s32[1,32,3]{1,0,2:T(1,128)}, u32[]{:S(2)}) copy-start(s32[1,32,3]{1,0,2:T(1,128)} %param.6) | copy-start | bytes 1156
  209.5 5.8 %copy-start.1 = (s32[1,8]{1,0:T(1,128)S(1)}, s32[1,8]{1,0:T(1,128)}, u32[]{:S(2)}) copy-start(s32[1,8]{1,0:T(1,128)} %param.7) | copy-start | bytes 100
  209.5 215.1 %all-to-all-start.1 = ((bf16[8,4096,128]{2,1,0:T(8,128)(2,1)}), bf16[8,4096,128]{2,1,0:T(8,128)(2,1)}, u32[]{:S(2)}, u32[]{:S(2)}) async-start(bf16[8,4096,128]{2,1,0:T(8,128)(2,1)} %shard_map.46), calls=%async_computation.1 | async-start | bytes 16777216 | tf_op jit(solution)/shard_map/all_to_all | solution.py:249
  214.6 69.9 %reduce-scatter.4.cloned.1.call-start = ((), (), s32[]{:S(2)}) async-start(), calls=%async_computation.4 | async-start | bytes 2027520
  216.2 68.3 %copy-start.2 = (s32[4]{0:T(128)S(1)}, s32[4]{0:T(128)}, u32[]{:S(2)}) copy-start(s32[4]{0:T(128)} %get-tuple-element.5.follows) | copy-start | bytes 52
  216.2 68.3 %copy-start.3 = (s32[4]{0:T(128)S(1)}, s32[4]{0:T(128)}, u32[]{:S(2)}) copy-start(s32[4]{0:T(128)} %get-tuple-element.6.leads) | copy-start | bytes 52
  250.5 157.9 %all-reduce.3.cloned.1.call-start = ((), (), s32[]{:S(2)}) async-start(), calls=%async_computation.3 | async-start | bytes 811008 | tf_op jit(solution)/shard_map/psum | solution.py:253
  408.4 1.0 copy-start
Sparse Core Ops, SparseCore 0:
  250.6 33.8 reduce-scatter.3
  287.0 121.3 all-reduce.2

commit v3 on v2

--- a/solution.py
+++ b/solution.py
@@ -15,20 +15,22 @@
     out_ref[...] = in_ref[...]
 
 
-def permute_blocks(blocks, index):
-    count, rows, cols = blocks.shape
+def permute_blocks(blocks, index, start, size):
+    count, _, cols = blocks.shape
     return pl.pallas_call(
         permute_kernel,
-        out_shape=jax.ShapeDtypeStruct(blocks.shape, blocks.dtype),
+        out_shape=jax.ShapeDtypeStruct((count, size, cols), blocks.dtype),
         grid_spec=pltpu.PrefetchScalarGridSpec(
             num_scalar_prefetch=1,
-            grid=(count, 2),
-            in_specs=[pl.BlockSpec((1, rows // 2, cols), lambda o, i, index: (index[o], i, 0))],
-            out_specs=pl.BlockSpec((1, rows // 2, cols), lambda o, i, index: (o, i, 0)),
+            grid=(count,),
+            in_specs=[
+                pl.BlockSpec((1, size, cols), lambda o, index: (index[o], start // size, 0))
+            ],
+            out_specs=pl.BlockSpec((1, size, cols), lambda o, index: (o, 0, 0)),
         ),
         compiler_params=pltpu.CompilerParams(vmem_limit_bytes=VMEM_LIMIT),
         cost_estimate=pl.CostEstimate(
-            flops=0, bytes_accessed=2 * blocks.size * 2, transcendentals=0
+            flops=0, bytes_accessed=4 * count * size * cols, transcendentals=0
         ),
     )(index, blocks)
 
@@ -201,31 +203,36 @@
     )(grams)
 
 
-def rotate_kernel(own_ref, other_ref, weight_ref, out_ref):
-    both = jnp.concatenate([own_ref[...], other_ref[...]], axis=1)
-    out_ref[...] = jnp.dot(both, weight_ref[...], preferred_element_type=jnp.float32).astype(
-        jnp.bfloat16
-    )
-
-
-def rotate(own, other, weight):
-    rows, half = own.shape
-    step = min(rows, 2048)
+def rotate_kernel(own_ref, other_ref, weight_ref, *refs):
+    out_ref = refs[-1]
+    count, rows, half = own_ref.shape
+    both = jnp.concatenate([own_ref[...], other_ref[...]], axis=2).reshape(count * rows, 2 * half)
+    out = jnp.dot(both, weight_ref[...], preferred_element_type=jnp.float32)
+    out_ref[...] = out.astype(jnp.bfloat16).reshape(count, rows, half)
+
+
+def rotate(own, other, weight, start, size, step, done=None):
+    groups, _, half = own.shape
+    at = start // size
     return pl.pallas_call(
         rotate_kernel,
         out_shape=jax.ShapeDtypeStruct(own.shape, own.dtype),
-        grid=(rows // step,),
+        grid=(groups // step,),
         in_specs=[
-            pl.BlockSpec((step, half), lambda i: (i, 0)),
-            pl.BlockSpec((step, half), lambda i: (i, 0)),
+            pl.BlockSpec((step, size, half), lambda i: (i, at, 0)),
+            pl.BlockSpec((step, size, half), lambda i: (i, 0, 0)),
             pl.BlockSpec((2 * half, half), lambda i: (0, 0)),
-        ],
-        out_specs=pl.BlockSpec((step, half), lambda i: (i, 0)),
+        ]
+        + ([] if done is None else [pl.BlockSpec(memory_space=pl.ANY)]),
+        out_specs=pl.BlockSpec((step, size, half), lambda i: (i, at, 0)),
+        input_output_aliases={} if done is None else {3: 0},
         compiler_params=pltpu.CompilerParams(vmem_limit_bytes=VMEM_LIMIT),
         cost_estimate=pl.CostEstimate(
-            flops=4 * rows * half * half, bytes_accessed=6 * own.size, transcendentals=0
-        ),
-    )(own, other, weight)
+            flops=4 * groups * size * half * half,
+            bytes_accessed=6 * groups * size * half,
+            transcendentals=0,
+        ),
+    )(own, other, weight, *([] if done is None else [done]))
 
 
 def body(coeffs, dipole, tile_cols, matching):
@@ -242,15 +249,19 @@
     leads = jnp.sum(jnp.where(chosen, block_ids[None, :], 0), axis=1)
     follows = jnp.sum(jnp.where(chosen, partner[None, :], 0), axis=1)
 
-    local = lax.all_to_all(
-        coeffs.reshape(blocks, rows // blocks, half), "orb", split_axis=0, concat_axis=0
-    )
-    swapped = permute_blocks(local, partner)
-    other = lax.all_to_all(swapped, "orb", split_axis=0, concat_axis=0).reshape(rows, half)
+    own = coeffs.reshape(blocks, rows // blocks, half)
+    last = rows // blocks // 4
+    first = 3 * last
+    local = lax.all_to_all(own, "orb", split_axis=0, concat_axis=0)
+    swapped = permute_blocks(local, partner, 0, first)
+    other_first = lax.all_to_all(swapped, "orb", split_axis=0, concat_axis=0)
 
     grams = pair_grams(local, dipole[:, 0], tile_cols[0], leads, follows)
     grams = lax.psum_scatter(grams, "bas", scatter_dimension=0, tiled=True)
     grams = lax.psum(grams, "orb")
+    swapped = permute_blocks(local, partner, first, last)
+    swapped, grams = lax.optimization_barrier((swapped, grams))
+    other_last = lax.all_to_all(swapped, "orb", split_axis=0, concat_axis=0)
     rotors = lax.all_gather(jacobi(grams), "bas", axis=0, tiled=True)
     mine = (leads == me) | (follows == me)
     rotor = jnp.sum(jnp.where(mine[:, None, None], rotors, jnp.zeros_like(rotors)), axis=0)
@@ -260,7 +271,9 @@
         rotor[:, :half],
         jnp.concatenate([rotor[half:, half:], rotor[:half, half:]], axis=0),
     )
-    return rotate(coeffs, other, weight)
+    out = rotate(own, other_first, weight, 0, first, 1)
+    out = rotate(own, other_last, weight, first, last, blocks // 2, out)
+    return out.reshape(rows, half)
 
 
 def solution(mesh):

time: 449 us -> 431 us (0.960)
  waiting for transfers between devices: 157 us -> 134 us
  starting transfers between devices: 5.18 us -> 9.77 us
    psum x1, waiting for transfers between devices: 123 us -> 78.3 us  [body(): grams = lax.psum(grams, 'orb')]
    all_to_all x1 -> x2, waiting for transfers between devices: 0.01 us -> 21.6 us  [the longest x1 21.6 us: body(): other_last = lax.all_to_all(swapped, 'orb', split_axis=0, concat_axis=0)]
    all_to_all x1 -> x2, starting transfers between devices: 5.1 us -> 9.69 us  [the longest x1 4.93 us: body(): other_first = lax.all_to_all(swapped, 'orb', split_axis=0, concat_axis=0)]
    pallas_call x1 -> x2, Pallas kernels: 12.6 us -> 14.8 us  [permute_blocks(): pl.pallas_call(permute_kernel, out_shape=jax.ShapeDtypeStruct((count, siz...]
    pallas_call x1 -> x2, Pallas kernels: 16.4 us -> 14.9 us  [rotate(): pl.pallas_call(rotate_kernel, out_shape=jax.ShapeDtypeStruct(own.shape, o...]
  transfers between devices with their start and end apart: 3 -> 4, of which waited for: 2 -> 3; matrix products, arithmetic and copies ran while one was open for 1% -> 1% of each run, Pallas kernels for 8% -> 13%
where the time goes in v3:
time: 431 us
  blocking collectives  201 us (47%)
  waiting for transfers between devices  134 us (31%)
  Pallas kernels  66.6 us (15%)
  between operations  13.5 us (3%)
  starting transfers between devices  9.77 us (2%)
    all_to_all x1, blocking collectives, body(): local = lax.all_to_all(own, 'orb', split_axis=0, concat_axis=0)  190 us
    psum x1, waiting for transfers between devices, body(): grams = lax.psum(grams, 'orb')  78.3 us
    pallas_call x1, Pallas kernels, pair_grams(): pl.pallas_call(functools.partial(pair_kernel, tiles, slots), out_shape=ja...  34.1 us
    unnamed x3, waiting for transfers between devices  33.9 us
    all_to_all x1, waiting for transfers between devices, body(): other_last = lax.all_to_all(swapped, 'orb', split_axis=0, concat_axis=0)  21.6 us
    pallas_call x2, Pallas kernels, rotate(): pl.pallas_call(rotate_kernel, out_shape=jax.ShapeDtypeStruct(own.shape, o...  14.9 us
    pallas_call x2, Pallas kernels, permute_blocks(): pl.pallas_call(permute_kernel, out_shape=jax.ShapeDtypeStruct((count, siz...  14.8 us
    all_gather x1, blocking collectives, body(): rotors = lax.all_gather(jacobi(grams), 'bas', axis=0, tiled=True)  10.7 us
  transfers between devices with their start and end apart: 4, of which 3 were waited for; matrix products, arithmetic and copies ran while one was open for 1% of the time, Pallas kernels for 13%

profile of v3, /device:TPU:0, one launch (start us, length us, event | category | flops | bytes accessed | tf_op | source)
XLA Modules:
  0.0 430.6 jit_solution(15082647249279665087)
XLA Ops:
  6.5 190.4 %all_to_all.15.in_ref.lead_ref.follow_ref = bf16[8,4096,128]{2,1,0:T(8,128)(2,1)} all-to-all(bf16[8,4096,128]{2,1,0:T(8,128)(2,1)} %bitcast.7), channel_id=1, replica_groups=mesh['orb'=8,'bas'=4] {'orb'}, dimensions={0} | all-to-all | bytes 16777216 | tf_op jit(solution)/shard_map/all_to_all | solution.py:255
  196.9 8.5 %shard_map.49 = bf16[8,3072,128]{2,1,0:T(8,128)(2,1)} custom-call(s32[8]{0:T(128)} %bitcast.10, bf16[8,4096,128]{2,1,0:T(8,128)(2,1)} %all_to_all.15.in_ref.lead_ref.follow_ref), custom_call_target="tpu_custom_call" | custom-call | bytes 12582912 | tf_op jit(solution)/shard_map/pallas_call | solution.py:20
  205.4 0.0 copy-start.5
  205.4 4.9 %all-to-all-start.2 = ((bf16[8,3072,128]{2,1,0:T(8,128)(2,1)}), bf16[8,3072,128]{2,1,0:T(8,128)(2,1)}, u32[]{:S(2)}, u32[]{:S(2)}) async-start(bf16[8,3072,128]{2,1,0:T(8,128)(2,1)} %shard_map.49), calls=%async_computation.2 | async-start | bytes 12582912 | tf_op jit(solution)/shard_map/all_to_all | solution.py:257
  210.4 0.0 reduce-scatter.4.cloned.1.call-start
  210.4 0.0 copy-done.5
  210.4 0.1 copy.9
  210.5 0.6 reshape_squeeze.3.table
  211.1 0.0 copy-done.2
  211.1 0.1 convert_reduce_fusion
  211.3 0.7 select_reduce_fusion.1
  212.0 34.1 %shard_map.47 = f32[4,3,264,128]{3,2,1,0:T(8,128)} custom-call(s32[4]{0:T(128)} %get-tuple-element.10.leads, s32[4]{0:T(128)} %get-tuple-element.9.follows, s32[96]{0:T(128)} %reshape_squeeze.3.table, bf16[8,4096,128]{2,1,0:T(8,128)(2,1)} %all_to_all.15.in_ref.lead_ref.follow_ref, bf16[8,4096,128]{2,1,0:T(8,128)(2,1)} %all_to_all.15.in_ref.lead_ref.follow_ref, ...), custom_call_target="tpu_custom_call" | custom-call | flops 16106127360 | bytes 17825792 | tf_op jit(solution)/shard_map/pallas_call | solution.py:85
  246.1 0.0 reduce-scatter.4.cloned.1.call-update
  246.1 0.0 all-reduce.3.cloned.1.call-start
  246.1 33.9 %reduce-scatter.4.cloned.1.call-done = f32[1,3,264,128]{3,2,1,0:T(8,128)} async-done(((f32[4,3,264,128]{3,2,1,0:T(8,128)}), f32[1,3,264,128]{3,2,1,0:T(8,128)}) %reduce-scatter.4.cloned.1.call-update) | async-done | bytes 405520
  280.0 0.0 all-reduce.3.cloned.1.call-update
  280.0 6.3 %shard_map.46 = bf16[8,1024,128]{2,1,0:T(8,128)(2,1)} custom-call(s32[8]{0:T(128)} %bitcast.11, bf16[8,4096,128]{2,1,0:T(8,128)(2,1)} %all_to_all.15.in_ref.lead_ref.follow_ref), custom_call_target="tpu_custom_call" | custom-call | bytes 4194304 | tf_op jit(solution)/shard_map/pallas_call | solution.py:20
  286.4 78.3 %all-reduce.3.cloned.1.call-done.in_ref = f32[1,3,264,128]{3,2,1,0:T(8,128)} async-done(((f32[1,3,264,128]{3,2,1,0:T(8,128)}), f32[1,3,264,128]{3,2,1,0:T(8,128)}) %all-reduce.3.cloned.1.call-update) | async-done | bytes 405520 | tf_op jit(solution)/shard_map/psum | solution.py:261
  364.6 0.0 all-to-all-done.2.other_ref
  364.6 4.8 %all-to-all-start.1 = ((bf16[8,1024,128]{2,1,0:T(8,128)(2,1)}), bf16[8,1024,128]{2,1,0:T(8,128)(2,1)S(1)}, u32[]{:S(2)}, u32[]{:S(2)}) async-start(bf16[8,1024,128]{2,1,0:T(8,128)(2,1)} %shard_map.46), calls=%async_computation.1 | async-start | bytes 4194304 | tf_op jit(solution)/shard_map/all_to_all | solution.py:264
  369.4 0.0 copy-done.3
  369.4 0.0 copy-done.4
  369.4 0.6 compare_reduce_fusion
  370.0 1.0 copy-done
  371.0 2.7 shard_map.48
  373.8 10.7 %all_gather.3 = bf16[4,256,256]{2,1,0:T(8,128)(2,1)S(1)} all-gather(bf16[1,256,256]{2,1,0:T(8,128)(2,1)S(1)} %shard_map.48), channel_id=1, replica_groups=mesh['orb'=8,'bas'=4] {'bas'}, dimensions={0}, use_global_device_ids=true | all-gather | bytes 655360 | tf_op jit(solution)/shard_map/all_gather | solution.py:265
  384.4 0.1 select_reduce_fusion
  384.6 1.3 slice_select_fusion.weight_ref
  385.9 11.0 %shard_map.50.refs_0_ = bf16[8,4096,128]{2,1,0:T(8,128)(2,1)} custom-call(bf16[8,4096,128]{2,1,0:T(8,128)(2,1)} %bitcast.8, bf16[8,3072,128]{2,1,0:T(8,128)(2,1)} %all-to-all-done.2.other_ref, bf16[256,128]{1,0:T(8,128)(2,1)} %slice_select_fusion.weight_ref), custom_call_target="tpu_custom_call" | custom-call | flops 1610612736 | bytes 18874368 | tf_op jit(solution)/shard_map/pallas_call | solution.py:217
  396.8 21.6 %all-to-all-done.1.other_ref = bf16[8,1024,128]{2,1,0:T(8,128)(2,1)S(1)} async-done(((bf16[8,1024,128]{2,1,0:T(8,128)(2,1)}), bf16[8,1024,128]{2,1,0:T(8,128)(2,1)S(1)}, u32[]{:S(2)}, u32[]{:S(2)}) %all-to-all-start.1) | async-done | bytes 2097184 | tf_op jit(solution)/shard_map/all_to_all | solution.py:264
  418.5 1.3 copy-done.1
  419.8 4.0 shard_map.51
  (7 shorter events, 0.0 us)
Async XLA Ops:
  205.4 5.0 %copy-start.5 = (s32[1,32,3]{1,0,2:T(1,128)S(1)}, s32[1,32,3]{1,0,2:T(1,128)}, u32[]{:S(2)}) copy-start(s32[1,32,3]{1,0,2:T(1,128)} %param.6) | copy-start | bytes 1156
  205.4 5.7 %copy-start.2 = (s32[1,8]{1,0:T(1,128)S(1)}, s32[1,8]{1,0:T(1,128)}, u32[]{:S(2)}) copy-start(s32[1,8]{1,0:T(1,128)} %param.7) | copy-start | bytes 100
  205.4 159.2 %all-to-all-start.2 = ((bf16[8,3072,128]{2,1,0:T(8,128)(2,1)}), bf16[8,3072,128]{2,1,0:T(8,128)(2,1)}, u32[]{:S(2)}, u32[]{:S(2)}) async-start(bf16[8,3072,128]{2,1,0:T(8,128)(2,1)} %shard_map.49), calls=%async_computation.2 | async-start | bytes 12582912 | tf_op jit(solution)/shard_map/all_to_all | solution.py:257
  210.4 69.6 %reduce-scatter.4.cloned.1.call-start = ((), (), s32[]{:S(2)}) async-start(), calls=%async_computation.5 | async-start | bytes 2027520
  246.1 123.3 %copy-start.3 = (s32[4]{0:T(128)S(1)}, s32[4]{0:T(128)}, u32[]{:S(2)}) copy-start(s32[4]{0:T(128)} %get-tuple-element.9.follows) | copy-start | bytes 52
  246.1 123.3 %copy-start.4 = (s32[4]{0:T(128)S(1)}, s32[4]{0:T(128)}, u32[]{:S(2)}) copy-start(s32[4]{0:T(128)} %get-tuple-element.10.leads) | copy-start | bytes 52
  246.1 118.5 %all-reduce.3.cloned.1.call-start = ((), (), s32[]{:S(2)}) async-start(), calls=%async_computation.4 | async-start | bytes 811008 | tf_op jit(solution)/shard_map/psum | solution.py:261
  364.6 53.8 %all-to-all-start.1 = ((bf16[8,1024,128]{2,1,0:T(8,128)(2,1)}), bf16[8,1024,128]{2,1,0:T(8,128)(2,1)S(1)}, u32[]{:S(2)}, u32[]{:S(2)}) async-start(bf16[8,1024,128]{2,1,0:T(8,128)(2,1)} %shard_map.46), calls=%async_computation.1 | async-start | bytes 4194304 | tf_op jit(solution)/shard_map/all_to_all | solution.py:264
  370.0 1.0 copy-start
  418.5 1.4 copy-start.1
Sparse Core Ops, SparseCore 0:
  246.2 33.7 reduce-scatter.3
  282.5 82.1 all-reduce.2

commit v4 on v3

--- a/solution.py
+++ b/solution.py
@@ -250,8 +250,8 @@
     follows = jnp.sum(jnp.where(chosen, partner[None, :], 0), axis=1)
 
     own = coeffs.reshape(blocks, rows // blocks, half)
-    last = rows // blocks // 4
-    first = 3 * last
+    last = rows // blocks // 8
+    first = 7 * last
     local = lax.all_to_all(own, "orb", split_axis=0, concat_axis=0)
     swapped = permute_blocks(local, partner, 0, first)
     other_first = lax.all_to_all(swapped, "orb", split_axis=0, concat_axis=0)

time: 431 us -> 427 us (level)
  waiting for transfers between devices: 134 us -> 129 us
    all_to_all x1, waiting for transfers between devices: 21.6 us -> 0.01 us  [body(): other_last = lax.all_to_all(swapped, 'orb', split_axis=0, concat_axis=0)]
    psum x1, waiting for transfers between devices: 78.3 us -> 95.3 us  [body(): grams = lax.psum(grams, 'orb')]
  transfers between devices with their start and end apart: 4 -> 4, of which waited for: 3 -> 2; matrix products, arithmetic and copies ran while one was open for 1% -> 1% of each run, Pallas kernels for 13% -> 13%
where the time goes in v4:
time: 427 us; the launch traced here: 426 us
  blocking collectives  203 us (48%)
  waiting for transfers between devices  129 us (30%)
  Pallas kernels  66.6 us (16%)
  between operations  13.5 us (3%)
  starting transfers between devices  8.68 us (2%)
    all_to_all x1, blocking collectives, body(): local = lax.all_to_all(own, 'orb', split_axis=0, concat_axis=0)  190 us
    psum x1, waiting for transfers between devices, body(): grams = lax.psum(grams, 'orb')  95.3 us
    pallas_call x1, Pallas kernels, pair_grams(): pl.pallas_call(functools.partial(pair_kernel, tiles, slots), out_shape=ja...  34.1 us
    unnamed x3, waiting for transfers between devices  33.9 us
    pallas_call x2, Pallas kernels, permute_blocks(): pl.pallas_call(permute_kernel, out_shape=jax.ShapeDtypeStruct((count, siz...  14.9 us
    pallas_call x2, Pallas kernels, rotate(): pl.pallas_call(rotate_kernel, out_shape=jax.ShapeDtypeStruct(own.shape, o...  14.9 us
    all_gather x1, blocking collectives, body(): rotors = lax.all_gather(jacobi(grams), 'bas', axis=0, tiled=True)  12.2 us
  transfers between devices with their start and end apart: 4, of which 2 were waited for; matrix products, arithmetic and copies ran while one was open for 1% of the time, Pallas kernels for 13%

profile of v4, /device:TPU:0, one launch (start us, length us, event | category | flops | bytes accessed | tf_op | source)
XLA Modules:
  0.0 426.4 jit_solution(14917973170889957248)
XLA Ops:
  6.5 190.4 %all_to_all.15.in_ref.lead_ref.follow_ref = bf16[8,4096,128]{2,1,0:T(8,128)(2,1)} all-to-all(bf16[8,4096,128]{2,1,0:T(8,128)(2,1)} %bitcast.7), channel_id=1, replica_groups=mesh['orb'=8,'bas'=4] {'orb'}, dimensions={0} | all-to-all | bytes 16777216 | tf_op jit(solution)/shard_map/all_to_all | solution.py:255
  196.9 9.0 %shard_map.49 = bf16[8,3584,128]{2,1,0:T(8,128)(2,1)} custom-call(s32[8]{0:T(128)} %bitcast.10, bf16[8,4096,128]{2,1,0:T(8,128)(2,1)} %all_to_all.15.in_ref.lead_ref.follow_ref), custom_call_target="tpu_custom_call" | custom-call | bytes 14680064 | tf_op jit(solution)/shard_map/pallas_call | solution.py:20
  206.0 0.0 copy-start.5
  206.0 5.0 %all-to-all-start.2 = ((bf16[8,3584,128]{2,1,0:T(8,128)(2,1)}), bf16[8,3584,128]{2,1,0:T(8,128)(2,1)}, u32[]{:S(2)}, u32[]{:S(2)}) async-start(bf16[8,3584,128]{2,1,0:T(8,128)(2,1)} %shard_map.49), calls=%async_computation.2 | async-start | bytes 14680064 | tf_op jit(solution)/shard_map/all_to_all | solution.py:257
  211.0 0.0 reduce-scatter.4.cloned.1.call-start
  211.1 0.0 copy-done.5
  211.1 0.1 copy.9
  211.2 0.7 reshape_squeeze.3.table
  211.9 0.0 copy-done.2
  211.9 0.1 convert_reduce_fusion
  212.0 0.8 select_reduce_fusion.1
  212.8 34.1 %shard_map.47 = f32[4,3,264,128]{3,2,1,0:T(8,128)} custom-call(s32[4]{0:T(128)} %get-tuple-element.10.leads, s32[4]{0:T(128)} %get-tuple-element.9.follows, s32[96]{0:T(128)} %reshape_squeeze.3.table, bf16[8,4096,128]{2,1,0:T(8,128)(2,1)} %all_to_all.15.in_ref.lead_ref.follow_ref, bf16[8,4096,128]{2,1,0:T(8,128)(2,1)} %all_to_all.15.in_ref.lead_ref.follow_ref, ...), custom_call_target="tpu_custom_call" | custom-call | flops 16106127360 | bytes 17825792 | tf_op jit(solution)/shard_map/pallas_call | solution.py:85
  246.9 0.0 reduce-scatter.4.cloned.1.call-update
  246.9 0.0 all-reduce.3.cloned.1.call-start
  246.9 33.9 %reduce-scatter.4.cloned.1.call-done = f32[1,3,264,128]{3,2,1,0:T(8,128)} async-done(((f32[4,3,264,128]{3,2,1,0:T(8,128)}), f32[1,3,264,128]{3,2,1,0:T(8,128)}) %reduce-scatter.4.cloned.1.call-update) | async-done | bytes 405520
  280.8 0.0 all-reduce.3.cloned.1.call-update
  280.8 5.9 %shard_map.46 = bf16[8,512,128]{2,1,0:T(8,128)(2,1)} custom-call(s32[8]{0:T(128)} %bitcast.11, bf16[8,4096,128]{2,1,0:T(8,128)(2,1)} %all_to_all.15.in_ref.lead_ref.follow_ref), custom_call_target="tpu_custom_call" | custom-call | bytes 2097152 | tf_op jit(solution)/shard_map/pallas_call | solution.py:20
  286.7 95.3 %all-reduce.3.cloned.1.call-done.in_ref = f32[1,3,264,128]{3,2,1,0:T(8,128)} async-done(((f32[1,3,264,128]{3,2,1,0:T(8,128)}), f32[1,3,264,128]{3,2,1,0:T(8,128)}) %all-reduce.3.cloned.1.call-update) | async-done | bytes 405520 | tf_op jit(solution)/shard_map/psum | solution.py:261
  382.0 0.0 all-to-all-done.2.other_ref
  382.0 3.6 all-to-all-start.1
  385.6 0.0 copy-done.3
  385.6 0.0 copy-done.4
  385.6 0.6 compare_reduce_fusion
  386.3 1.0 copy-done
  387.3 2.7 shard_map.48
  390.0 12.2 %all_gather.3 = bf16[4,256,256]{2,1,0:T(8,128)(2,1)S(1)} all-gather(bf16[1,256,256]{2,1,0:T(8,128)(2,1)S(1)} %shard_map.48), channel_id=1, replica_groups=mesh['orb'=8,'bas'=4] {'bas'}, dimensions={0}, use_global_device_ids=true | all-gather | bytes 655360 | tf_op jit(solution)/shard_map/all_gather | solution.py:265
  402.2 0.1 select_reduce_fusion
  402.4 1.3 slice_select_fusion.weight_ref
  403.7 12.0 %shard_map.50.refs_0_ = bf16[8,4096,128]{2,1,0:T(8,128)(2,1)} custom-call(bf16[8,4096,128]{2,1,0:T(8,128)(2,1)} %bitcast.8, bf16[8,3584,128]{2,1,0:T(8,128)(2,1)} %all-to-all-done.2.other_ref, bf16[256,128]{1,0:T(8,128)(2,1)} %slice_select_fusion.weight_ref), custom_call_target="tpu_custom_call" | custom-call | flops 1879048192 | bytes 22020096 | tf_op jit(solution)/shard_map/pallas_call | solution.py:217
  415.7 0.0 all-to-all-done.1.other_ref
  415.7 1.0 copy-done.1
  416.7 2.9 shard_map.51
  (7 shorter events, 0.0 us)
Async XLA Ops:
  206.0 5.1 %copy-start.5 = (s32[1,32,3]{1,0,2:T(1,128)S(1)}, s32[1,32,3]{1,0,2:T(1,128)}, u32[]{:S(2)}) copy-start(s32[1,32,3]{1,0,2:T(1,128)} %param.6) | copy-start | bytes 1156
  206.0 5.9 %copy-start.2 = (s32[1,8]{1,0:T(1,128)S(1)}, s32[1,8]{1,0:T(1,128)}, u32[]{:S(2)}) copy-start(s32[1,8]{1,0:T(1,128)} %param.7) | copy-start | bytes 100
  206.0 176.1 %all-to-all-start.2 = ((bf16[8,3584,128]{2,1,0:T(8,128)(2,1)}), bf16[8,3584,128]{2,1,0:T(8,128)(2,1)}, u32[]{:S(2)}, u32[]{:S(2)}) async-start(bf16[8,3584,128]{2,1,0:T(8,128)(2,1)} %shard_map.49), calls=%async_computation.2 | async-start | bytes 14680064 | tf_op jit(solution)/shard_map/all_to_all | solution.py:257
  211.0 69.8 %reduce-scatter.4.cloned.1.call-start = ((), (), s32[]{:S(2)}) async-start(), calls=%async_computation.5 | async-start | bytes 2027520
  246.9 138.8 %copy-start.3 = (s32[4]{0:T(128)S(1)}, s32[4]{0:T(128)}, u32[]{:S(2)}) copy-start(s32[4]{0:T(128)} %get-tuple-element.9.follows) | copy-start | bytes 52
  246.9 138.8 %copy-start.4 = (s32[4]{0:T(128)S(1)}, s32[4]{0:T(128)}, u32[]{:S(2)}) copy-start(s32[4]{0:T(128)} %get-tuple-element.10.leads) | copy-start | bytes 52
  246.9 135.1 %all-reduce.3.cloned.1.call-start = ((), (), s32[]{:S(2)}) async-start(), calls=%async_computation.4 | async-start | bytes 811008 | tf_op jit(solution)/shard_map/psum | solution.py:261
  382.0 33.6 %all-to-all-start.1 = ((bf16[8,512,128]{2,1,0:T(8,128)(2,1)}), bf16[8,512,128]{2,1,0:T(8,128)(2,1)S(1)}, u32[]{:S(2)}, u32[]{:S(2)}) async-start(bf16[8,512,128]{2,1,0:T(8,128)(2,1)} %shard_map.46), calls=%async_computation.1 | async-start | bytes 2097152 | tf_op jit(solution)/shard_map/all_to_all | solution.py:264
  386.3 1.0 copy-start
  415.7 1.0 copy-start.1
Sparse Core Ops, SparseCore 0:
  247.0 33.7 reduce-scatter.3
  283.3 98.7 all-reduce.2
